TPU v7x, 32 devices: a whole 2x2x4 slice. The times are simulated.
32 devices in a mesh: node: 4 (over y, x), freq: 8 (over z, core).
Axes of the slice: x: 2, y: 2, z: 4, core: 2. Of those that a mesh axis runs over, the one named last changes fastest.
Arguments:
- first_vector: float32 [2, 256, 512, 256], P(None, 'freq', 'node'), may hold values from -6 to 6
- second_vector: float32 [2, 256, 512, 256], P(None, 'freq', 'node'), may hold values from -6 to 6
- conductance: float32 [2, 256, 512, 256], P(None, 'freq', 'node'), may hold values from 0.1 to 2
- terminals: int32 [512, 3], replicated, may hold values from 0 to 127
- pattern: int32 [16, 3], P('node'), may hold values from 0 to 3, all different within a row
- conduct_blocks: float32 [16, 3, 32, 32], P('node'), may hold values from -0.625 to 0.625
- capacit_blocks: float32 [16, 3, 32, 32], P('node'), may hold values from -0.625 to 0.625
Outputs:
- first_product: float32 [2, 256, 512, 256], P(None, 'freq', 'node')
- second_product: float32 [2, 256, 512, 256], P(None, 'freq', 'node')
Inputs may be any that keep to these rules, and one draw needn't show every extreme that they name: `terminals`: drain and source indices count within the transistor's own node block; transistor j of a node block (j counted within the block) takes its gate from node block j // 32, so every node block draws exactly 32 gates from every node block. `pattern`: each row names 3 different column blocks, counted within the row's own node block.
All inputs are finite; a program needn't handle non-finite values.
Results may differ from a plain program's by a relative error of at most 0.000058.
Values sent between devices are 32-bit elements; how exact they have to be, the bound alone decides.
A program may use at most 192 MiB of HBM per device.

v0:
```python
import math

import jax
import jax.numpy as jnp
from jax import lax
from jax.sharding import PartitionSpec as P

precise = lax.Precision.HIGHEST


def contract(form, left, right):
    return jnp.einsum(form, left, right, precision=precise)


def cos_sin(first, second, length):
    angle = (first[:, None] * second[None, :] % length).astype(jnp.float32) * (
        2.0 * math.pi / length
    )
    return (jnp.cos(angle), jnp.sin(angle))


def body(
    first_vector, second_vector, conductance, terminals, pattern, conduct_blocks, capacit_blocks
):
    freq_count = lax.axis_size("freq")
    groups = lax.axis_size("node")
    local_bins = first_vector.shape[1]
    node_dev = first_vector.shape[2]
    inner_size = first_vector.shape[3]
    outer_size = local_bins * freq_count
    samples = outer_size * inner_size
    local_steps = inner_size // freq_count
    capacity = node_dev // groups
    freq_index = lax.axis_index("freq")
    node_index = lax.axis_index("node")
    bin_first = freq_index * local_bins + jnp.arange(local_bins, dtype=jnp.int32)
    step_first = freq_index * local_steps + jnp.arange(local_steps, dtype=jnp.int32)
    inner_range = jnp.arange(inner_size, dtype=jnp.int32)
    outer_range = jnp.arange(outer_size, dtype=jnp.int32)
    inner_cos, inner_sin = cos_sin(inner_range, inner_range, inner_size)
    outer_cos, outer_sin = cos_sin(outer_range, outer_range, outer_size)
    back_cos, back_sin = cos_sin(inner_range, bin_first, samples)
    fore_cos, fore_sin = cos_sin(step_first, outer_range, samples)

    def inverse_second(spread):
        real_part, imag_part = (spread[0], spread[1])
        sig_real = contract("man,al->mln", real_part, outer_cos) - contract(
            "man,al->mln", imag_part, outer_sin
        )
        sig_imag = contract("man,al->mln", real_part, outer_sin) + contract(
            "man,al->mln", imag_part, outer_cos
        )
        return jnp.stack([sig_real, sig_imag]) / samples

    def forward_second(collected):
        real_part, imag_part = (collected[0], collected[1])
        out_real = contract("man,mb->anb", real_part, inner_cos) + contract(
            "man,mb->anb", imag_part, inner_sin
        )
        out_imag = contract("man,mb->anb", imag_part, inner_cos) - contract(
            "man,mb->anb", real_part, inner_sin
        )
        return jnp.stack([out_real, out_imag])

    vectors = (first_vector, second_vector)
    signals = []
    for vector in vectors:
        inverse_real_part = vector[0]
        inverse_imag_part = vector[1]
        mixed_real = contract("anb,bm->man", inverse_real_part, inner_cos) - contract(
            "anb,bm->man", inverse_imag_part, inner_sin
        )
        mixed_imag = contract("anb,bm->man", inverse_real_part, inner_sin) + contract(
            "anb,bm->man", inverse_imag_part, inner_cos
        )
        inverse_twist_cos = back_cos[:, :, None]
        inverse_twist_sin = back_sin[:, :, None]
        spread = lax.all_to_all(
            jnp.stack(
                [
                    mixed_real * inverse_twist_cos - mixed_imag * inverse_twist_sin,
                    mixed_real * inverse_twist_sin + mixed_imag * inverse_twist_cos,
                ]
            ),
            "freq",
            split_axis=1,
            concat_axis=2,
            tiled=True,
        )
        signals.append(inverse_second(spread))
    signal = jnp.stack(signals)
    own_rows = lax.dynamic_slice_in_dim(terminals, node_index * node_dev, node_dev, 0)
    node_ids = jnp.arange(node_dev, dtype=jnp.int32)
    drain_hot = (node_ids[:, None] == own_rows[None, :, 0]).astype(jnp.float32)
    source_hot = (node_ids[:, None] == own_rows[None, :, 1]).astype(jnp.float32)
    at_drain = contract("vcmln,nd->vcmdl", signal, drain_hot)
    at_source = contract("vcmln,nd->vcmdl", signal, source_hot)
    arranged = terminals.reshape(groups, groups, capacity, 3)
    wanted = lax.dynamic_index_in_dim(arranged, node_index, axis=1, keepdims=False)
    gate_hot = (node_ids[None, :, None] == wanted[:, None, :, 2]).astype(jnp.float32)
    outgoing = contract("vcmln,rnp->rvcmpl", signal, gate_hot)
    incoming = lax.all_to_all(outgoing, "node", split_axis=0, concat_axis=0, tiled=True)
    moved = incoming.transpose(1, 2, 3, 0, 4, 5)
    at_gate = moved.reshape(
        moved.shape[0], moved.shape[1], moved.shape[2], node_dev, moved.shape[5]
    )
    trans_g = conductance[0]
    output_g = conductance[1]
    current = trans_g * (at_gate - at_source) + output_g * (at_drain - at_source)
    incidence = drain_hot - source_hot
    stamped = contract("vcmdl,nd->vcmln", current, incidence)
    responses = []
    for which in range(2):
        stamped_one = stamped[which]
        forward_real_part = stamped_one[0]
        forward_imag_part = stamped_one[1]
        turn_real = contract("mln,la->man", forward_real_part, outer_cos) + contract(
            "mln,la->man", forward_imag_part, outer_sin
        )
        turn_imag = contract("mln,la->man", forward_imag_part, outer_cos) - contract(
            "mln,la->man", forward_real_part, outer_sin
        )
        twist_cos = fore_cos[:, :, None]
        twist_sin = fore_sin[:, :, None]
        collected = lax.all_to_all(
            jnp.stack(
                [
                    turn_real * twist_cos + turn_imag * twist_sin,
                    turn_imag * twist_cos - turn_real * twist_sin,
                ]
            ),
            "freq",
            split_axis=2,
            concat_axis=1,
            tiled=True,
        )
        responses.append(forward_second(collected))
    block_size = conduct_blocks.shape[2]
    block_count = node_dev // block_size
    pattern_hot = (
        pattern[:, :, None] == jnp.arange(block_count, dtype=jnp.int32)[None, None, :]
    ).astype(jnp.float32)
    conduct_dense = contract("bjc,bjrs->brcs", pattern_hot, conduct_blocks).reshape(
        node_dev, node_dev
    )
    capacit_dense = contract("bjc,bjrs->brcs", pattern_hot, capacit_blocks).reshape(
        node_dev, node_dev
    )
    bin_index = bin_first[:, None] + outer_size * inner_range[None, :]
    signed = jnp.where(bin_index < samples // 2, bin_index, bin_index - samples)
    angular = (signed.astype(jnp.float32) * (2.0 * math.pi / samples))[:, None, :]
    results = []
    for which in range(2):
        vector = vectors[which]
        real_out = contract("rs,asb->arb", conduct_dense, vector[0]) - angular * contract(
            "rs,asb->arb", capacit_dense, vector[1]
        )
        imag_out = contract("rs,asb->arb", conduct_dense, vector[1]) + angular * contract(
            "rs,asb->arb", capacit_dense, vector[0]
        )
        results.append(jnp.stack([real_out, imag_out]) + responses[which])
    return (results[0], results[1])


def solution(mesh):
    return jax.shard_map(
        body,
        mesh=mesh,
        in_specs=(
            P(None, "freq", "node", None),
            P(None, "freq", "node", None),
            P(None, "freq", "node", None),
            P(),
            P("node", None),
            P("node", None, None, None),
            P("node", None, None, None),
        ),
        out_specs=(P(None, "freq", "node", None), P(None, "freq", "node", None)),
        check_vma=False,
    )
```

profile of v0, /device:TPU:0, one launch (start us, length us, event | category | flops | bytes accessed | tf_op | source)
XLA Modules:
  0.0 1302.0 jit_solution(2359972610788668271)
XLA Ops:
  0.7 11.8 fusion.42
  12.5 11.8 fusion.40
  24.3 10.4 fusion.30
  34.7 10.2 fusion.28
  45.1 11.5 fusion.88
  56.6 11.1 fusion.91
  67.8 7.9 fusion.94
  75.7 13.8 %subtract_bitcast_fusion.6 = (f32[1,256,32,128]{3,1,2,0:T(8,128)}, f32[1,256,32,128]{3,1,2,0:T(8,128)}, f32[1,256,32,128]{3,1,2,0:T(8,128)S(1)}, f32[1,256,32,128]{3,1,2,0:T(8,128)}) fusion(f32[256,32,128]{2,0,1:T(8,128)S(1)} %fusion.91, f32[256,32,128]{2,0,1:T(8,128)S(1)} %fusion.88, f32[256,32]{0,1:T(8,128)S(1)} %get-tuple-element.30, ...), kind=kOutput, calls=%fused_computation.91 | convolution fusion | flops 3235774464 | bytes 37814272 | tf_op jit(solution)/shard_map/anb,bm->man/dot_general | solution.py:12
  92.2 8.3 copy.148
  100.5 6.8 all-to-all-start.1
  111.3 8.3 copy.138
  119.5 171.7 %all-to-all-done.1 = f32[2,256,32,128]{3,2,0,1:T(8,128)} async-done(((f32[2,256,32,128]{3,2,0,1:T(8,128)}), f32[2,256,32,128]{3,2,0,1:T(8,128)}, u32[]{:S(2)}, u32[]{:S(2)}) %all-to-all-start.1) | async-done | bytes 8388640 | tf_op jit(solution)/shard_map/all_to_all | solution.py:78
  291.2 5.0 all-to-all-start
  304.1 7.0 fusion.139
  311.2 7.3 fusion.115
  318.4 161.7 %all-to-all-done = f32[2,256,32,128]{3,2,0,1:T(8,128)} async-done(((f32[2,256,32,128]{3,2,0,1:T(8,128)}), f32[2,256,32,128]{3,2,0,1:T(8,128)}, u32[]{:S(2)}, u32[]{:S(2)}) %all-to-all-start) | async-done | bytes 8388640 | tf_op jit(solution)/shard_map/all_to_all | solution.py:78
  486.3 5.2 fusion.144
  491.6 4.8 fusion.120
  496.4 5.0 subtract_bitcast_fusion.3
  501.4 7.1 add_bitcast_fusion.3
  508.5 7.2 subtract_bitcast_fusion.5
  515.7 7.4 add_bitcast_fusion.5
  523.2 7.5 maximum_multiply_fusion
  534.1 14.7 %fusion.11 = f32[4,2,2,32,32,256]{5,4,3,2,1,0:T(8,128)} fusion(f32[1,2,32,256,128]{4,3,2,1,0:T(8,128)} %get-tuple-element.32, f32[1,2,32,256,128]{4,3,2,1,0:T(8,128)S(1)} %get-tuple-element.31, s32[4,32]{1,0:T(4,128)S(1)} %slice_bitcast_fusion.22), kind=kOutput, calls=%fused_computation.12 | convolution fusion | flops 6446661632 | bytes 33554944 | tf_op jit(solution)/shard_map/vcmln,rnp->rvcmpl/dot_general | solution.py:12
  548.8 7.3 all-to-all-start.2
  556.4 7.9 slice_bitcast_fusion.5
  564.3 14.1 %fusion.10 = f32[128,2,2,32,256]{4,0,3,2,1:T(8,128)} fusion(f32[1,2,32,256,128]{4,3,2,1,0:T(8,128)} %get-tuple-element.32, f32[1,2,32,256,128]{4,3,2,1,0:T(8,128)S(1)} %copy-done.3, s32[128]{0:T(128)S(1)} %get-tuple-element.24), kind=kOutput, calls=%fused_computation.11 | convolution fusion | flops 6446678016 | bytes 33554944 | tf_op jit(solution)/shard_map/vcmln,nd->vcmdl/dot_general | solution.py:12
  578.4 14.0 %fusion.9 = f32[128,2,2,32,256]{4,0,3,2,1:T(8,128)} fusion(f32[1,2,32,256,128]{4,3,2,1,0:T(8,128)} %get-tuple-element.32, f32[1,2,32,256,128]{4,3,2,1,0:T(8,128)S(1)} %copy-done.3, s32[128]{0:T(128)S(1)} %get-tuple-element.25), kind=kOutput, calls=%fused_computation.10 | convolution fusion | flops 6446678016 | bytes 33554944 | tf_op jit(solution)/shard_map/vcmln,nd->vcmdl/dot_general | solution.py:12
  592.4 146.0 %all-to-all-done.2 = f32[4,2,2,32,32,256]{5,4,3,2,1,0:T(8,128)} async-done(((f32[4,2,2,32,32,256]{5,4,3,2,1,0:T(8,128)}), f32[4,2,2,32,32,256]{5,4,3,2,1,0:T(8,128)}, u32[]{:S(2)}, u32[]{:S(2)}) %all-to-all-start.2) | async-done | bytes 16777248 | tf_op jit(solution)/shard_map/all_to_all | solution.py:102
  738.4 13.0 copy.154
  751.4 35.6 %fusion.2 = f32[2,2,32,256,128]{4,3,2,1,0:T(8,128)} fusion(f32[128,2,2,32,256]{4,0,3,2,1:T(8,128)} %fusion.9, f32[128,2,2,32,256]{4,0,3,2,1:T(8,128)} %fusion.10, f32[2,2,32,128,256]{4,3,2,1,0:T(8,128)} %bitcast.390, f32[32,128,256]{2,1,0:T(8,128)S(1)} %copy-done.5, f32[32,128,256]{2,1,0:T(8,128)S(1)} %copy-done.4, s32[128]{0:T(128)S(1)} %get-tuple-element.25, ...), kind=kOutput, calls=%fused_computation.4 | convolution fusion | flops 6463504384 | bytes 75498496 | tf_op jit(solution)/shard_map/vcmdl,nd->vcmln/dot_general | solution.py:12
  786.9 7.5 fusion.57
  794.4 7.7 fusion.61
  802.2 4.8 fusion.60
  807.0 7.2 fusion.56
  814.2 5.2 fusion.82
  819.4 5.2 fusion.80
  824.6 5.9 fusion.81
  830.5 13.7 %fusion.17 = (f32[1,32,256,128]{3,2,1,0:T(8,128)}, f32[1,32,256,128]{3,2,1,0:T(8,128)}, f32[1,32,256,128]{3,2,1,0:T(8,128)}, f32[1,32,256,128]{3,2,1,0:T(8,128)}) fusion(f32[256,32,128]{2,0,1:T(8,128)S(1)} %fusion.81, f32[256,32,128]{2,0,1:T(8,128)S(1)} %fusion.80, f32[32,256]{1,0:T(8,128)S(1)} %get-tuple-element.27, f32[32,256]{1,0:T(8,128)S(1)} %get-tuple-element.26, ...), kind=kOutput, calls=%fused_computation.32 | convolution fusion | flops 3235774464 | bytes 37814272 | tf_op jit(solution)/shard_map/mln,la->man/dot_general | solution.py:12
  848.3 8.3 copy.174
  856.5 5.1 all-to-all-start.4
  865.7 8.3 copy.162
  873.9 171.6 %all-to-all-done.4 = f32[2,32,256,128]{3,1,0,2:T(8,128)} async-done(((f32[2,32,256,128]{3,1,0,2:T(8,128)}), f32[2,32,256,128]{3,1,0,2:T(8,128)}, u32[]{:S(2)}, u32[]{:S(2)}) %all-to-all-start.4) | async-done | bytes 8388640 | tf_op jit(solution)/shard_map/all_to_all | solution.py:125
  1045.5 5.0 all-to-all-start.3
  1051.8 5.5 fusion.24
  1057.4 8.2 add_bitcast_fusion.1
  1069.4 5.8 subtract_bitcast_fusion.1
  1078.9 5.3 add_bitcast_fusion.7
  1088.0 5.6 subtract_bitcast_fusion.7
  1093.6 8.2 copy.175
  1107.7 5.3 copy.177
  1117.7 5.3 copy.179
  1123.0 7.5 fusion.129
  1130.6 6.9 add_bitcast_fusion
  1141.9 7.3 subtract_bitcast_fusion
  1149.3 85.2 %all-to-all-done.3 = f32[2,32,256,128]{3,1,0,2:T(8,128)} async-done(((f32[2,32,256,128]{3,1,0,2:T(8,128)}), f32[2,32,256,128]{3,1,0,2:T(8,128)}, u32[]{:S(2)}, u32[]{:S(2)}) %all-to-all-start.3) | async-done | bytes 8388640 | tf_op jit(solution)/shard_map/all_to_all | solution.py:125
  1234.4 8.2 copy.163
  1248.6 5.4 copy.165
  1254.0 8.7 fusion.133
  1265.4 5.3 copy.167
  1270.6 7.5 fusion.131
  1282.7 7.0 subtract_bitcast_fusion.2
  1289.8 4.9 maximum_add_fusion.1
  1296.1 5.7 maximum_add_fusion
  (106 shorter events, 74.7 us)
Async XLA Ops:
  0.6 1049.9 %copy-start = (f32[4,3,32,32]{3,2,1,0:T(8,128)S(1)}, f32[4,3,32,32]{3,2,1,0:T(8,128)}, u32[]{:S(2)}) copy-start(f32[4,3,32,32]{3,2,1,0:T(8,128)} %param.12) | copy-start | bytes 147460
  0.6 23.6 %slice-start = ((s8[8388608]{0:T(1024)(128)(4,1)}), s8[4194304]{0:T(1024)(128)(4,1)S(1)}, s32[]{:S(2)}) async-start(s8[8388608]{0:T(1024)(128)(4,1)} %bitcast.382), calls=%async_computation.5 | async-start | bytes 8388608
  12.5 11.8 slice-start.1
  45.1 11.6 copy-start.15
  45.1 22.7 %slice-start.2 = ((s8[8388608]{0:T(1024)(128)(4,1)}), s8[4194304]{0:T(1024)(128)(4,1)S(1)}, s32[]{:S(2)}) async-start(s8[8388608]{0:T(1024)(128)(4,1)} %bitcast.384), calls=%async_computation.7 | async-start | bytes 8388608
  56.6 11.1 slice-start.3
  56.6 11.1 copy-start.13
  67.8 7.9 copy-start.11
  100.5 190.7 %all-to-all-start.1 = ((f32[2,256,32,128]{3,2,0,1:T(8,128)}), f32[2,256,32,128]{3,2,0,1:T(8,128)}, u32[]{:S(2)}, u32[]{:S(2)}) async-start(f32[2,256,32,128]{3,2,0,1:T(8,128)} %copy.148), calls=%async_computation.1 | async-start | bytes 16777216 | tf_op jit(solution)/shard_map/all_to_all | solution.py:78
  119.5 176.7 %copy-start.25 = (s32[512,3]{0,1:T(4,128)S(1)}, s32[512,3]{0,1:T(4,128)}, u32[]{:S(2)}) copy-start(s32[512,3]{0,1:T(4,128)} %param.10) | copy-start | bytes 18436
  291.2 188.9 %all-to-all-start = ((f32[2,256,32,128]{3,2,0,1:T(8,128)}), f32[2,256,32,128]{3,2,0,1:T(8,128)}, u32[]{:S(2)}, u32[]{:S(2)}) async-start(f32[2,256,32,128]{3,2,0,1:T(8,128)} %copy.138), calls=%async_computation | async-start | bytes 16777216 | tf_op jit(solution)/shard_map/all_to_all | solution.py:78
  491.5 4.9 copy-start.6
  491.6 4.9 copy-start.14
  496.4 5.0 copy-start.12
  530.7 3.4 copy-start.2
  548.8 189.6 %all-to-all-start.2 = ((f32[4,2,2,32,32,256]{5,4,3,2,1,0:T(8,128)}), f32[4,2,2,32,32,256]{5,4,3,2,1,0:T(8,128)}, u32[]{:S(2)}, u32[]{:S(2)}) async-start(f32[4,2,2,32,32,256]{5,4,3,2,1,0:T(8,128)} %fusion.11), calls=%async_computation.2 | async-start | bytes 33554432 | tf_op jit(solution)/shard_map/all_to_all | solution.py:102
  556.3 7.9 copy-start.3
  738.4 13.0 copy-start.4
  738.4 13.0 copy-start.5
  786.9 15.2 %copy-start.1 = (f32[2,2,32,256,128]{4,3,2,1,0:T(8,128)S(1)}, f32[2,2,32,256,128]{4,3,2,1,0:T(8,128)}, u32[]{:S(2)}) copy-start(f32[2,2,32,256,128]{4,3,2,1,0:T(8,128)} %fusion.2) | copy-start | bytes 50331652
  856.5 189.0 %all-to-all-start.4 = ((f32[2,32,256,128]{3,1,0,2:T(8,128)}), f32[2,32,256,128]{3,1,0,2:T(8,128)}, u32[]{:S(2)}, u32[]{:S(2)}) async-start(f32[2,32,256,128]{3,1,0,2:T(8,128)} %copy.174), calls=%async_computation.4 | async-start | bytes 16777216 | tf_op jit(solution)/shard_map/all_to_all | solution.py:125
  873.9 176.6 %copy-start.26 = (s32[4,3]{1,0:T(4,128)S(1)}, s32[4,3]{1,0:T(4,128)}, u32[]{:S(2)}) copy-start(s32[4,3]{1,0:T(4,128)} %param.11) | copy-start | bytes 148
  873.9 177.3 %copy-start.24 = (f32[4,3,32,32]{3,2,1,0:T(8,128)S(1)}, f32[4,3,32,32]{3,2,1,0:T(8,128)}, u32[]{:S(2)}) copy-start(f32[4,3,32,32]{3,2,1,0:T(8,128)} %param.13) | copy-start | bytes 147460
  1045.5 188.9 %all-to-all-start.3 = ((f32[2,32,256,128]{3,1,0,2:T(8,128)}), f32[2,32,256,128]{3,1,0,2:T(8,128)}, u32[]{:S(2)}, u32[]{:S(2)}) async-start(f32[2,32,256,128]{3,1,0,2:T(8,128)} %copy.162), calls=%async_computation.3 | async-start | bytes 16777216 | tf_op jit(solution)/shard_map/all_to_all | solution.py:125
  1051.8 13.8 %slice-start.4 = ((s8[8388608]{0:T(1024)(128)(4,1)}), s8[4194304]{0:T(1024)(128)(4,1)S(1)}, s32[]{:S(2)}) async-start(s8[8388608]{0:T(1024)(128)(4,1)} %bitcast.386), calls=%async_computation.9 | async-start | bytes 8388608
  1057.4 8.3 slice-start.5
  1065.6 9.5 slice-start.6
  1069.4 5.8 slice-start.7
  1123.0 7.5 copy-start.9
  1137.5 4.4 copy-start.7
  1254.0 8.8 copy-start.23
  1270.6 7.6 copy-start.10
  1270.6 7.6 copy-start.16
  1278.2 4.4 copy-start.8
  1278.2 11.5 copy-start.22
  1282.7 7.1 copy-start.17
  1282.7 7.1 copy-start.19
  1282.7 7.1 copy-start.21
  1289.7 4.9 copy-start.18
  1289.8 6.4 copy-start.20
where the time goes:
time: 1310 us; the launch traced here: 1300 us
  waiting for transfers between devices  736 us (56%)
  matrix products  372 us (28%)
  local copies, waits for them, and re-layouts  130 us (10%)
  other arithmetic  33.2 us (3%)
  starting transfers between devices  29.2 us (2%)
    dot_general x46, matrix products, contract(): return jnp.einsum(form, left, right, precision=precise)  372 us
    all_to_all x2, waiting for transfers between devices, body(): lax.all_to_all(jnp.stack([mixed_real * inverse_twist_cos - mixed_imag * i...  333 us
    all_to_all x2, waiting for transfers between devices, body(): lax.all_to_all(jnp.stack([turn_real * twist_cos + turn_imag * twist_sin,...  257 us
    all_to_all x1, waiting for transfers between devices, body(): lax.all_to_all(outgoing, 'node', split_axis=0, concat_axis=0, tiled=True)  146 us
  transfers between devices with their start and end apart: 5, of which 5 were waited for; matrix products, arithmetic and copies ran while one was open for 14% of the time, Pallas kernels for 0%

commit v1 on v0

v1 whole, which is shorter than its diff:
```python
import math

import jax
import jax.numpy as jnp
from jax import lax
from jax.sharding import PartitionSpec as P

precise = lax.Precision.HIGH


def contract(form, left, right):
    return jnp.einsum(form, left, right, precision=precise)


def cos_sin(first, second, length):
    angle = (first[:, None] * second[None, :] % length).astype(jnp.float32) * (
        2.0 * math.pi / length
    )
    return (jnp.cos(angle), jnp.sin(angle))


def body(
    first_vector, second_vector, conductance, terminals, pattern, conduct_blocks, capacit_blocks
):
    freq_count = lax.axis_size("freq")
    groups = lax.axis_size("node")
    local_bins = first_vector.shape[1]
    node_dev = first_vector.shape[2]
    inner_size = first_vector.shape[3]
    outer_size = local_bins * freq_count
    samples = outer_size * inner_size
    local_steps = inner_size // freq_count
    capacity = node_dev // groups
    freq_index = lax.axis_index("freq")
    node_index = lax.axis_index("node")
    bin_first = freq_index * local_bins + jnp.arange(local_bins, dtype=jnp.int32)
    step_first = freq_index * local_steps + jnp.arange(local_steps, dtype=jnp.int32)
    inner_range = jnp.arange(inner_size, dtype=jnp.int32)
    outer_range = jnp.arange(outer_size, dtype=jnp.int32)
    inner_cos, inner_sin = cos_sin(inner_range, inner_range, inner_size)
    outer_cos, outer_sin = cos_sin(outer_range, outer_range, outer_size)
    back_cos, back_sin = cos_sin(inner_range, bin_first, samples)
    fore_cos, fore_sin = cos_sin(step_first, outer_range, samples)

    def wave(cos, sin):
        return jnp.stack(
            [jnp.stack([cos, sin], axis=1), jnp.stack([-sin, cos], axis=1)], axis=0
        )

    inner_back = wave(inner_cos, inner_sin)
    outer_back = wave(outer_cos, outer_sin) / samples
    inner_fore = wave(inner_cos, -inner_sin)
    outer_fore = wave(outer_cos, -outer_sin)

    def inverse_first(vector):
        mixed = contract("canb,cbem->eman", vector, inner_back)
        cos, sin = back_cos[:, :, None], back_sin[:, :, None]
        return jnp.stack(
            [mixed[0] * cos - mixed[1] * sin, mixed[0] * sin + mixed[1] * cos]
        )

    def inverse_exchange(twisted):
        return lax.all_to_all(twisted, "freq", split_axis=1, concat_axis=2, tiled=True)

    def inverse_second(spread):
        return contract("cman,cael->emnl", spread, outer_back)

    def forward_first(current):
        stamped = contract("cmdl,nd->cmnl", current, incidence)
        turned = contract("cmnl,clea->eman", stamped, outer_fore)
        cos, sin = fore_cos[:, :, None], fore_sin[:, :, None]
        return jnp.stack(
            [turned[0] * cos + turned[1] * sin, turned[1] * cos - turned[0] * sin]
        )

    def forward_exchange(twisted):
        return lax.all_to_all(twisted, "freq", split_axis=2, concat_axis=1, tiled=True)

    def forward_second(collected):
        return contract("cman,cmeb->eanb", collected, inner_fore)

    def arrange(values, axis):
        return jnp.concatenate(
            [
                lax.dynamic_slice_in_dim(values, (node_index ^ s) * capacity, capacity, axis)
                for s in range(groups)
            ],
            axis=axis,
        )

    own_rows = arrange(
        lax.dynamic_slice_in_dim(terminals, node_index * node_dev, node_dev, 0), 0
    )
    node_ids = jnp.arange(node_dev, dtype=jnp.int32)
    drain_hot = (node_ids[:, None] == own_rows[None, :, 0]).astype(jnp.float32)
    source_hot = (node_ids[:, None] == own_rows[None, :, 1]).astype(jnp.float32)
    incidence = drain_hot - source_hot
    arranged = terminals.reshape(groups, groups, capacity, 3)
    wanted = lax.dynamic_index_in_dim(arranged, node_index, axis=1, keepdims=False)
    conduct = arrange(conductance, 2)
    trans_g, output_g = conduct[0], conduct[1]

    def middle(signal):
        blocks = []
        for s in range(groups):
            rows = lax.dynamic_index_in_dim(wanted, node_index ^ s, 0, keepdims=False)
            hot = (node_ids[:, None] == rows[None, :, 2]).astype(jnp.float32)
            block = contract("cmnl,np->cmpl", signal, hot)
            if s:
                pairs = [(g, g ^ s) for g in range(groups)]
                block = lax.ppermute(block, "node", pairs)
            blocks.append(block)
        at_source = contract("cmnl,nd->cmdl", signal, source_hot)
        across = contract("cmnl,nd->cmdl", signal, incidence)
        at_gate = jnp.concatenate(blocks, axis=2)
        return trans_g * (at_gate - at_source) + output_g * across

    block_size = conduct_blocks.shape[2]
    block_count = node_dev // block_size
    pattern_hot = (
        pattern[:, :, None] == jnp.arange(block_count, dtype=jnp.int32)[None, None, :]
    ).astype(jnp.float32)

    def dense(blocks):
        return jnp.einsum(
            "bjc,bjrs->brcs", pattern_hot, blocks, precision=lax.Precision.HIGHEST
        ).reshape(node_dev, node_dev)

    conduct_dense = dense(conduct_blocks)
    capacit_dense = dense(capacit_blocks)
    bin_index = bin_first[:, None] + outer_size * inner_range[None, :]
    signed = jnp.where(bin_index < samples // 2, bin_index, bin_index - samples)
    angular = (signed.astype(jnp.float32) * (2.0 * math.pi / samples))[:, None, :]

    def linear(vector):
        real_out = contract("rs,asb->arb", conduct_dense, vector[0]) - angular * contract(
            "rs,asb->arb", capacit_dense, vector[1]
        )
        imag_out = contract("rs,asb->arb", conduct_dense, vector[1]) + angular * contract(
            "rs,asb->arb", capacit_dense, vector[0]
        )
        return jnp.stack([real_out, imag_out])

    twisted_one = inverse_first(first_vector)
    spread_one = inverse_exchange(twisted_one)
    later, _ = lax.optimization_barrier((second_vector, twisted_one))
    twisted_two = inverse_first(later)
    spread_one, twisted_two = lax.optimization_barrier((spread_one, twisted_two))
    spread_two = inverse_exchange(twisted_two)
    sent_one = forward_first(middle(inverse_second(spread_one)))
    spread_two, sent_one = lax.optimization_barrier((spread_two, sent_one))
    collected_one = forward_exchange(sent_one)
    sent_two = forward_first(middle(inverse_second(spread_two)))
    collected_one, sent_two = lax.optimization_barrier((collected_one, sent_two))
    collected_two = forward_exchange(sent_two)
    vector_one, vector_two, collected_one = lax.optimization_barrier(
        (first_vector, second_vector, collected_one)
    )
    first_product = linear(vector_one) + forward_second(collected_one)
    second_linear = linear(vector_two)
    second_product = second_linear + forward_second(collected_two)
    return (first_product, second_product)


def solution(mesh):
    return jax.shard_map(
        body,
        mesh=mesh,
        in_specs=(
            P(None, "freq", "node", None),
            P(None, "freq", "node", None),
            P(None, "freq", "node", None),
            P(),
            P("node", None),
            P("node", None, None, None),
            P("node", None, None, None),
        ),
        out_specs=(P(None, "freq", "node", None), P(None, "freq", "node", None)),
        check_vma=False,
    )
```

time: 1310 us -> 867 us (0.66)
  waiting for transfers between devices: 736 us -> 509 us
  matrix products: 372 us -> 178 us
  local copies, waits for them, and re-layouts: 130 us -> 111 us
    all_to_all x5 -> x4, waiting for transfers between devices: 736 us -> 363 us  [the longest x2 203 us: inverse_exchange(): lax.all_to_all(twisted, 'freq', split_axis=1, concat_axis=2, tiled=True)]
    dot_general x46 -> x30, matrix products: 372 us -> 177 us  [contract(): return jnp.einsum(form, left, right, precision=precise)]
    ppermute x0 -> x6, waiting for transfers between devices: none -> 146 us  [middle(): block = lax.ppermute(block, 'node', pairs)]
    optimization_barrier x0 -> x5, local copies, waits for them, and re-layouts: none -> 42.4 us  [the longest x2 17.8 us: body(): lax.optimization_barrier((first_vector, second_vector, collected_one))]
    another operation x4 -> x1, local copies, waits for them, and re-layouts: 33 us -> 8.26 us  [inverse_first(): jnp.stack([mixed[0] * cos - mixed[1] * sin, mixed[0] * sin + mixed[1] * c...]
    slice x8 -> x0, local copies, waits for them, and re-layouts: 24.3 us -> none  [the longest x6 19.2 us: forward_second(): real_part, imag_part = (collected[0], collected[1])]
    squeeze x4 -> x2, local copies, waits for them, and re-layouts: 21.2 us -> 0.01 us  [middle(): rows = lax.dynamic_index_in_dim(wanted, node_index ^ s, 0, keepdims=False)]
    unnamed x70 -> x56, local copies, waits for them, and re-layouts: 5.06 us -> 20.8 us
  transfers between devices with their start and end apart: 5 -> 10, of which waited for: 5 -> 10; matrix products, arithmetic and copies ran while one was open for 14% -> 25% of each run, Pallas kernels for 0% -> 0%
where the time goes in v1:
time: 867 us; the launch traced here: 859 us
  waiting for transfers between devices  509 us (59%)
  matrix products  178 us (21%)
  local copies, waits for them, and re-layouts  111 us (13%)
  starting transfers between devices  29.6 us (3%)
  other arithmetic  29.3 us (3%)
    all_to_all x2, waiting for transfers between devices, inverse_exchange(): lax.all_to_all(twisted, 'freq', split_axis=1, concat_axis=2, tiled=True)  203 us
    dot_general x30, matrix products, contract(): return jnp.einsum(form, left, right, precision=precise)  177 us
    all_to_all x2, waiting for transfers between devices, forward_exchange(): lax.all_to_all(twisted, 'freq', split_axis=2, concat_axis=1, tiled=True)  160 us
    ppermute x6, waiting for transfers between devices, middle(): block = lax.ppermute(block, 'node', pairs)  146 us
    unnamed x56, local copies, waits for them, and re-layouts  20.8 us
    optimization_barrier x2, local copies, waits for them, and re-layouts, body(): lax.optimization_barrier((first_vector, second_vector, collected_one))  17.8 us
  transfers between devices with their start and end apart: 10, of which 10 were waited for; matrix products, arithmetic and copies ran while one was open for 25% of the time, Pallas kernels for 0%

profile of v1, /device:TPU:0, one launch (start us, length us, event | category | flops | bytes accessed | tf_op | source)
XLA Modules:
  0.0 858.8 jit_solution(9143587543541572320)
XLA Ops:
  4.1 9.5 %fusion.56 = f32[2,256,32,128]{3,1,2,0:T(8,128)S(1)} fusion(f32[2,32,128,256]{3,2,1,0:T(8,128)} %param.7, f32[1,256,2,256]{1,3,0,2:T(8,128)S(1)} %get-tuple-element.41, f32[1,256,2,256]{1,3,0,2:T(8,128)S(1)} %get-tuple-element.44), kind=kOutput, calls=%fused_computation.85 | convolution fusion | flops 6442713088 | bytes 17825792 | tf_op jit(solution)/shard_map/canb,cbem->eman/dot_general | solution.py:12
  13.6 2.8 multiply_subtract_fusion.3
  17.4 8.3 copy.34
  25.6 6.8 all-to-all-start
  32.5 9.1 %fusion.59 = f32[2,256,32,128]{3,1,2,0:T(8,128)S(1)} fusion(f32[2,32,128,256]{3,2,1,0:T(8,128)} %param.8, f32[1,256,2,256]{1,3,0,2:T(8,128)S(1)} %get-tuple-element.41, f32[1,256,2,256]{1,3,0,2:T(8,128)S(1)} %get-tuple-element.44), kind=kOutput, calls=%fused_computation.86 | convolution fusion | flops 6442713088 | bytes 17825792 | tf_op jit(solution)/shard_map/canb,cbem->eman/dot_general | solution.py:12
  41.6 2.8 multiply_subtract_fusion.2
  44.4 3.9 pad_maximum_fusion.1
  48.4 168.1 %all-to-all-done = f32[2,256,32,128]{3,2,0,1:T(8,128)} async-done(((f32[2,256,32,128]{3,2,0,1:T(8,128)}), f32[2,256,32,128]{3,2,0,1:T(8,128)}, u32[]{:S(2)}, u32[]{:S(2)}) %all-to-all-start) | async-done | bytes 8388640 | tf_op jit(solution)/shard_map/all_to_all | solution.py:63
  216.4 8.4 copy.35
  224.9 8.3 copy.37
  233.1 5.3 all-to-all-start.1
  239.6 6.6 constant_dynamic-slice_fusion.7
  246.2 9.3 %fusion.36 = f32[2,256,32,128,1]{3,1,4,2,0:T(8,128)S(1)} fusion(f32[2,32,256,128]{3,2,0,1:T(8,128)} %bitcast.336, f32[1,256,2,256]{1,3,0,2:T(8,128)S(1)} %get-tuple-element.41, f32[1,256,2,256]{1,3,0,2:T(8,128)S(1)} %get-tuple-element.44), kind=kOutput, calls=%fused_computation.47 | convolution fusion | flops 6442975232 | bytes 17825792 | tf_op jit(solution)/shard_map/cman,cael->emnl/dot_general | solution.py:12
  255.6 4.3 fusion.83
  259.9 2.4 collective-permute-start.2
  262.3 4.3 fusion.80
  267.1 4.4 fusion.77
  272.8 2.6 slice_bitcast_fusion.5
  275.4 4.2 fusion.74
  279.7 7.1 fusion.24
  286.8 22.8 %collective-permute-done.2 = f32[2,32,32,256]{3,2,1,0:T(8,128)} collective-permute-done((f32[2,32,32,256]{3,2,1,0:T(8,128)}, f32[2,32,32,256]{3,2,1,0:T(8,128)}, u32[]{:S(2)}, u32[]{:S(2)}) %collective-permute-start.2) | collective-permute-done | bytes 2097184 | tf_op jit(solution)/shard_map/ppermute | solution.py:111
  309.6 44.4 %collective-permute-done.1 = f32[2,32,32,256]{3,2,1,0:T(8,128)} collective-permute-done((f32[2,32,32,256]{3,2,1,0:T(8,128)}, f32[2,32,32,256]{3,2,1,0:T(8,128)}, u32[]{:S(2)}, u32[]{:S(2)}) %collective-permute-start.1) | collective-permute-done | bytes 2097184 | tf_op jit(solution)/shard_map/ppermute | solution.py:111
  354.1 11.5 %fusion.1 = f32[2,32,128,256]{3,2,1,0:T(8,128)} fusion(f32[2,32,32,256]{3,2,1,0:T(8,128)} %collective-permute-done.2, f32[2,32,32,256]{3,2,1,0:T(8,128)} %collective-permute-done.1, f32[2,32,32,256]{3,2,1,0:T(8,128)} %collective-permute-done, f32[2,32,32,256]{3,2,1,0:T(8,128)} %fusion.74, f32[128,2,32,256]{3,0,2,1:T(8,128)} %fusion.24, ...), kind=kOutput, calls=%fused_computation.5 | convolution fusion | flops 1625325568 | bytes 41943552 | tf_op jit(solution)/shard_map/cmnl,nd->cmdl/dot_general | solution.py:12
  365.6 6.8 fusion.44
  372.5 7.6 fusion.66
  380.1 3.0 multiply_add_fusion.1
  383.0 3.9 pad_maximum_fusion.3
  387.0 35.3 %all-to-all-done.1 = f32[2,256,32,128]{3,2,0,1:T(8,128)} async-done(((f32[2,256,32,128]{3,2,0,1:T(8,128)}), f32[2,256,32,128]{3,2,0,1:T(8,128)}, u32[]{:S(2)}, u32[]{:S(2)}) %all-to-all-start.1) | async-done | bytes 8388640 | tf_op jit(solution)/shard_map/all_to_all | solution.py:63
  422.3 8.4 copy.38
  430.7 8.3 copy.44
  439.0 5.1 all-to-all-start.2
  444.1 9.6 %fusion.22 = f32[2,256,32,128,1]{3,1,4,2,0:T(8,128)S(1)} fusion(f32[2,32,256,128]{3,2,0,1:T(8,128)} %bitcast.337, f32[1,256,2,256]{1,3,0,2:T(8,128)S(1)} %copy-done.15, f32[1,256,2,256]{1,3,0,2:T(8,128)S(1)} %copy-done.17), kind=kOutput, calls=%fused_computation.32 | convolution fusion | flops 6442975232 | bytes 17825792 | tf_op jit(solution)/shard_map/cman,cael->emnl/dot_general | solution.py:12
  453.7 2.9 fusion.89
  456.7 2.9 fusion.92
  459.6 2.9 fusion.95
  462.5 2.5 collective-permute-start.5
  466.1 4.3 fusion.86
  470.4 7.5 fusion.10
  478.0 34.2 %collective-permute-done.5 = f32[2,32,32,256]{3,2,1,0:T(8,128)} collective-permute-done((f32[2,32,32,256]{3,2,1,0:T(8,128)S(1)}, f32[2,32,32,256]{3,2,1,0:T(8,128)}, u32[]{:S(2)}, u32[]{:S(2)}) %collective-permute-start.5) | collective-permute-done | bytes 2097184 | tf_op jit(solution)/shard_map/ppermute | solution.py:111
  512.1 44.3 %collective-permute-done.4 = f32[2,32,32,256]{3,2,1,0:T(8,128)} collective-permute-done((f32[2,32,32,256]{3,2,1,0:T(8,128)S(1)}, f32[2,32,32,256]{3,2,1,0:T(8,128)}, u32[]{:S(2)}, u32[]{:S(2)}) %collective-permute-start.4) | collective-permute-done | bytes 2097184 | tf_op jit(solution)/shard_map/ppermute | solution.py:111
  556.6 11.5 %fusion.3 = f32[2,32,128,256]{3,2,1,0:T(8,128)} fusion(f32[2,32,32,256]{3,2,1,0:T(8,128)} %collective-permute-done.5, f32[2,32,32,256]{3,2,1,0:T(8,128)} %collective-permute-done.4, f32[2,32,32,256]{3,2,1,0:T(8,128)} %collective-permute-done.3, f32[2,32,32,256]{3,2,1,0:T(8,128)} %fusion.86, f32[128,2,32,256]{3,0,2,1:T(8,128)} %fusion.10, ...), kind=kOutput, calls=%fused_computation.9 | convolution fusion | flops 1625325568 | bytes 41943552 | tf_op jit(solution)/shard_map/cmnl,nd->cmdl/dot_general | solution.py:12
  568.1 6.4 fusion.42
  574.5 7.6 fusion.69
  582.1 3.0 multiply_add_fusion
  585.1 3.8 pad_maximum_fusion.4
  588.9 39.1 %all-to-all-done.2 = f32[2,32,256,128]{3,1,0,2:T(8,128)} async-done(((f32[2,32,256,128]{3,1,0,2:T(8,128)}), f32[2,32,256,128]{3,1,0,2:T(8,128)}, u32[]{:S(2)}, u32[]{:S(2)}) %all-to-all-start.2) | async-done | bytes 8388640 | tf_op jit(solution)/shard_map/all_to_all | solution.py:77
  628.0 8.4 copy.45
  636.5 8.1 copy.54
  644.6 5.3 all-to-all-start.3
  651.2 8.9 %copy.47 = f32[2,32,128,256]{2,3,1,0:T(8,128)} copy(f32[2,32,128,256]{3,2,1,0:T(8,128)} %param.7) | data formatting | bytes 16777216 | tf_op jit(solution)/shard_map/optimization_barrier | solution.py:156
  660.1 3.8 fusion.48
  664.7 2.5 add_bitcast_fusion.1
  667.2 1.8 fusion.49
  669.0 2.5 subtract_bitcast_fusion.1
  671.6 9.2 %maximum_add_fusion = f32[2,32,128,256]{2,3,1,0:T(8,128)} fusion(f32[1,32,128,256]{2,3,1,0:T(8,128)S(1)} %add_bitcast_fusion.1, f32[1,32,128,256]{2,3,1,0:T(8,128)S(1)} %subtract_bitcast_fusion.1, f32[2,256,32,128]{3,1,0,2:T(8,128)S(1)} %bitcast.334, f32[1,256,2,256]{1,3,2,0:T(8,128)S(1)} %copy-done.13, f32[1,256,2,256]{1,3,2,0:T(8,128)S(1)} %copy-done.11), kind=kOutput, calls=%fused_computation.11 | convolution fusion | flops 6446907392 | bytes 26214400 | tf_op jit(solution)/shard_map/cman,cmeb->eanb/dot_general | solution.py:12
  680.8 8.9 %copy.57 = f32[2,32,128,256]{3,2,1,0:T(8,128)} copy(f32[2,32,128,256]{2,3,1,0:T(8,128)} %maximum_add_fusion) | data formatting | bytes 16777216
  689.7 8.9 %copy.52 = f32[2,32,128,256]{2,3,1,0:T(8,128)} copy(f32[2,32,128,256]{3,2,1,0:T(8,128)} %param.8) | data formatting | bytes 16777216 | tf_op jit(solution)/shard_map/optimization_barrier | solution.py:156
  698.5 3.8 fusion.52
  703.2 4.0 add_bitcast_fusion
  709.0 3.9 subtract_bitcast_fusion
  712.9 120.9 %all-to-all-done.3 = f32[2,32,256,128]{3,1,0,2:T(8,128)} async-done(((f32[2,32,256,128]{3,1,0,2:T(8,128)}), f32[2,32,256,128]{3,1,0,2:T(8,128)}, u32[]{:S(2)}, u32[]{:S(2)}) %all-to-all-start.3) | async-done | bytes 8388640 | tf_op jit(solution)/shard_map/all_to_all | solution.py:77
  833.8 4.6 copy.55
  839.7 9.8 %maximum_add_fusion.1 = f32[2,32,128,256]{2,3,1,0:T(8,128)} fusion(f32[1,32,128,256]{2,3,1,0:T(8,128)S(1)} %copy-done.8, f32[1,32,128,256]{2,3,1,0:T(8,128)S(1)} %copy-done.9, f32[2,256,32,128,1]{3,1,0,2,4:T(8,128)S(1)} %bitcast.335, f32[1,256,2,256]{1,3,2,0:T(8,128)S(1)} %copy-done.13, f32[1,256,2,256]{1,3,2,0:T(8,128)S(1)} %copy-done.11), kind=kOutput, calls=%fused_computation.12 | convolution fusion | flops 6446907392 | bytes 26214400 | tf_op jit(solution)/shard_map/cman,cmeb->eanb/dot_general | solution.py:12
  849.4 8.9 %copy.58 = f32[2,32,128,256]{3,2,1,0:T(8,128)} copy(f32[2,32,128,256]{2,3,1,0:T(8,128)} %maximum_add_fusion.1) | data formatting | bytes 16777216
  (86 shorter events, 14.6 us)
Async XLA Ops:
  0.6 649.3 %copy-start = (f32[4,3,32,32]{3,2,1,0:T(8,128)S(1)}, f32[4,3,32,32]{3,2,1,0:T(8,128)}, u32[]{:S(2)}) copy-start(f32[4,3,32,32]{3,2,1,0:T(8,128)} %param.12) | copy-start | bytes 147460
  4.1 242.1 %copy-start.14 = (f32[1,256,2,256]{1,3,0,2:T(8,128)}, f32[1,256,2,256]{1,3,0,2:T(8,128)S(1)}, u32[]{:S(2)}) copy-start(f32[1,256,2,256]{1,3,0,2:T(8,128)S(1)} %get-tuple-element.41) | copy-start | bytes 1572868
  4.1 242.1 %copy-start.16 = (f32[1,256,2,256]{1,3,0,2:T(8,128)}, f32[1,256,2,256]{1,3,0,2:T(8,128)S(1)}, u32[]{:S(2)}) copy-start(f32[1,256,2,256]{1,3,0,2:T(8,128)S(1)} %get-tuple-element.44) | copy-start | bytes 1572868
  25.6 190.8 %all-to-all-start = ((f32[2,256,32,128]{3,2,0,1:T(8,128)}), f32[2,256,32,128]{3,2,0,1:T(8,128)}, u32[]{:S(2)}, u32[]{:S(2)}) async-start(f32[2,256,32,128]{3,2,0,1:T(8,128)} %copy.34), calls=%async_computation | async-start | bytes 16777216 | tf_op jit(solution)/shard_map/all_to_all | solution.py:63
  216.4 8.4 copy-start.5
  233.1 5.4 copy-start.23
  233.1 189.2 %all-to-all-start.1 = ((f32[2,256,32,128]{3,2,0,1:T(8,128)}), f32[2,256,32,128]{3,2,0,1:T(8,128)}, u32[]{:S(2)}, u32[]{:S(2)}) async-start(f32[2,256,32,128]{3,2,0,1:T(8,128)} %copy.37), calls=%async_computation.1 | async-start | bytes 16777216 | tf_op jit(solution)/shard_map/all_to_all | solution.py:63
  259.9 12.1 %copy-start.18 = (f32[2,32,32,256]{3,2,1,0:T(8,128)S(1)}, f32[2,32,32,256]{3,2,1,0:T(8,128)}, u32[]{:S(2)}) copy-start(f32[2,32,32,256]{3,2,1,0:T(8,128)} %get-tuple-element.37) | copy-start | bytes 6291460
  259.9 12.1 %copy-start.19 = (f32[2,32,32,256]{3,2,1,0:T(8,128)S(1)}, f32[2,32,32,256]{3,2,1,0:T(8,128)}, u32[]{:S(2)}) copy-start(f32[2,32,32,256]{3,2,1,0:T(8,128)} %get-tuple-element.38) | copy-start | bytes 6291460
  259.9 12.1 %copy-start.20 = (f32[2,32,32,256]{3,2,1,0:T(8,128)S(1)}, f32[2,32,32,256]{3,2,1,0:T(8,128)}, u32[]{:S(2)}) copy-start(f32[2,32,32,256]{3,2,1,0:T(8,128)} %get-tuple-element.39) | copy-start | bytes 6291460
  259.9 49.7 %collective-permute-start.2 = (f32[2,32,32,256]{3,2,1,0:T(8,128)}, f32[2,32,32,256]{3,2,1,0:T(8,128)}, u32[]{:S(2)}, u32[]{:S(2)}) collective-permute-start(f32[2,32,32,256]{3,2,1,0:T(8,128)} %fusion.83), channel_id=1, source_target_pairs={{0,24},{8,16},{16,8},{24,0},{1,25},{9,17},{17,9},{25,1},{2,26},{10... | collective-permute-start | bytes 6291464 | tf_op jit(solution)/shard_map/ppermute | solution.py:111
  266.6 87.4 %collective-permute-start.1 = (f32[2,32,32,256]{3,2,1,0:T(8,128)}, f32[2,32,32,256]{3,2,1,0:T(8,128)}, u32[]{:S(2)}, u32[]{:S(2)}) collective-permute-start(f32[2,32,32,256]{3,2,1,0:T(8,128)} %fusion.80), channel_id=1, source_target_pairs={{0,16},{8,24},{16,0},{24,8},{1,17},{9,25},{17,1},{25,9},{2,18},{10... | collective-permute-start | bytes 6291464 | tf_op jit(solution)/shard_map/ppermute | solution.py:111
  271.4 82.7 %collective-permute-start = (f32[2,32,32,256]{3,2,1,0:T(8,128)}, f32[2,32,32,256]{3,2,1,0:T(8,128)}, u32[]{:S(2)}, u32[]{:S(2)}) collective-permute-start(f32[2,32,32,256]{3,2,1,0:T(8,128)} %fusion.77), channel_id=1, source_target_pairs={{0,8},{8,0},{16,24},{24,16},{1,9},{9,1},{17,25},{25,17},{2,10},{10... | collective-permute-start | bytes 6291464 | tf_op jit(solution)/shard_map/ppermute | solution.py:111
  275.4 78.7 %copy-start.1 = (f32[32,128,256]{2,1,0:T(8,128)}, f32[32,128,256]{2,1,0:T(8,128)S(1)}, u32[]{:S(2)}) copy-start(f32[32,128,256]{2,1,0:T(8,128)S(1)} %get-tuple-element.34) | copy-start | bytes 12582916
  365.6 6.8 copy-start.10
  365.6 6.8 copy-start.12
  422.3 8.4 copy-start.6
  439.0 5.1 copy-start.15
  439.0 5.1 copy-start.17
  439.0 189.0 %all-to-all-start.2 = ((f32[2,32,256,128]{3,1,0,2:T(8,128)}), f32[2,32,256,128]{3,1,0,2:T(8,128)}, u32[]{:S(2)}, u32[]{:S(2)}) async-start(f32[2,32,256,128]{3,1,0,2:T(8,128)} %copy.44), calls=%async_computation.2 | async-start | bytes 16777216 | tf_op jit(solution)/shard_map/all_to_all | solution.py:77
  462.5 49.6 %collective-permute-start.5 = (f32[2,32,32,256]{3,2,1,0:T(8,128)S(1)}, f32[2,32,32,256]{3,2,1,0:T(8,128)}, u32[]{:S(2)}, u32[]{:S(2)}) collective-permute-start(f32[2,32,32,256]{3,2,1,0:T(8,128)S(1)} %fusion.95), channel_id=1, source_target_pairs={{0,24},{8,16},{16,8},{24,0},{1,25},{9,17},{17,9},{25,1},{2,26},{10... | collective-permute-start | bytes 6291464 | tf_op jit(solution)/shard_map/ppermute | solution.py:111
  465.1 91.4 %collective-permute-start.4 = (f32[2,32,32,256]{3,2,1,0:T(8,128)S(1)}, f32[2,32,32,256]{3,2,1,0:T(8,128)}, u32[]{:S(2)}, u32[]{:S(2)}) collective-permute-start(f32[2,32,32,256]{3,2,1,0:T(8,128)S(1)} %fusion.92), channel_id=1, source_target_pairs={{0,16},{8,24},{16,0},{24,8},{1,17},{9,25},{17,1},{25,9},{2,18},{10... | collective-permute-start | bytes 6291464 | tf_op jit(solution)/shard_map/ppermute | solution.py:111
  465.6 91.0 %collective-permute-start.3 = (f32[2,32,32,256]{3,2,1,0:T(8,128)S(1)}, f32[2,32,32,256]{3,2,1,0:T(8,128)}, u32[]{:S(2)}, u32[]{:S(2)}) collective-permute-start(f32[2,32,32,256]{3,2,1,0:T(8,128)S(1)} %fusion.89), channel_id=1, source_target_pairs={{0,8},{8,0},{16,24},{24,16},{1,9},{9,1},{17,25},{25,17},{2,10},{10... | collective-permute-start | bytes 6291464 | tf_op jit(solution)/shard_map/ppermute | solution.py:111
  470.4 86.1 %copy-start.2 = (f32[32,128,256]{2,1,0:T(8,128)S(1)}, f32[32,128,256]{2,1,0:T(8,128)}, u32[]{:S(2)}) copy-start(f32[32,128,256]{2,1,0:T(8,128)} %copy-done.1) | copy-start | bytes 12582916
  568.1 6.4 copy-start.11
  568.1 6.4 copy-start.13
  628.0 8.4 copy-start.7
  644.6 5.4 copy-start.24
  644.6 6.0 copy-start.22
  644.6 189.2 %all-to-all-start.3 = ((f32[2,32,256,128]{3,1,0,2:T(8,128)}), f32[2,32,256,128]{3,1,0,2:T(8,128)}, u32[]{:S(2)}, u32[]{:S(2)}) async-start(f32[2,32,256,128]{3,1,0,2:T(8,128)} %copy.54), calls=%async_computation.3 | async-start | bytes 16777216 | tf_op jit(solution)/shard_map/all_to_all | solution.py:77
  660.1 4.6 copy-start.4
  660.1 4.6 copy-start.21
  667.2 4.3 slice-start
  669.0 2.5 slice-start.1
  698.5 4.6 copy-start.3
  833.8 4.6 copy-start.8
  833.8 5.9 copy-start.9

commit v2 on v1

--- a/solution.py
+++ b/solution.py
@@ -3,6 +3,9 @@
 import jax
 import jax.numpy as jnp
 from jax import lax
+from jax.experimental import pallas as pl
+from jax.experimental.layout import Layout, with_layout_constraint
+from jax.experimental.pallas import tpu as pltpu
 from jax.sharding import PartitionSpec as P
 
 precise = lax.Precision.HIGH
@@ -17,6 +20,131 @@
         2.0 * math.pi / length
     )
     return (jnp.cos(angle), jnp.sin(angle))
+
+
+def split(values):
+    high = values.astype(jnp.bfloat16)
+    low = (values - high.astype(jnp.float32)).astype(jnp.bfloat16)
+    return high, low
+
+
+def dot(left, right):
+    return lax.dot_general(
+        left, right, (((0,), (0,)), ((), ())), preferred_element_type=jnp.float32
+    )
+
+
+def last_kernel(collected_ref, wave_ref, linear_ref, out_ref, high_ref, low_ref):
+    shards, bins, _, steps, nodes = collected_ref.shape
+    inner = shards * steps
+
+    @pl.when(pl.program_id(0) == 0)
+    def _():
+        high, low = split(wave_ref[...])
+        high_ref[...] = high
+        low_ref[...] = low
+
+    for t in range(0, bins, 2):
+        columns = [
+            jnp.concatenate(
+                [collected_ref[:, u, c].reshape(inner, nodes) for c in range(2)], axis=0
+            )
+            for u in (t, t + 1)
+        ]
+        high, low = split(jnp.concatenate(columns, axis=1))
+        total = dot(high, low_ref[...]) + dot(low, high_ref[...])
+        total = total + dot(high, high_ref[...])
+        for h in range(2):
+            rows = total[h * nodes : (h + 1) * nodes]
+            for e in range(2):
+                part = rows[:, e * inner : (e + 1) * inner]
+                out_ref[e, t + h] = linear_ref[e, t + h] + part
+
+
+def last_stage(collected, wave, linear):
+    shards, bins, _, steps, nodes = collected.shape
+    inner = shards * steps
+    tile = 4
+    return pl.pallas_call(
+        last_kernel,
+        grid=(bins // tile,),
+        in_specs=[
+            pl.BlockSpec((shards, tile, 2, steps, nodes), lambda i: (0, i, 0, 0, 0)),
+            pl.BlockSpec((2 * inner, 2 * inner), lambda i: (0, 0)),
+            pl.BlockSpec((2, tile, nodes, inner), lambda i: (0, i, 0, 0)),
+        ],
+        out_specs=pl.BlockSpec((2, tile, nodes, inner), lambda i: (0, i, 0, 0)),
+        out_shape=jax.ShapeDtypeStruct(linear.shape, jnp.float32),
+        scratch_shapes=[
+            pltpu.VMEM((2 * inner, 2 * inner), jnp.bfloat16),
+            pltpu.VMEM((2 * inner, 2 * inner), jnp.bfloat16),
+        ],
+        compiler_params=pltpu.CompilerParams(vmem_limit_bytes=32 * 1024 * 1024),
+        cost_estimate=pl.CostEstimate(
+            flops=6 * bins * nodes * 4 * inner * inner,
+            bytes_accessed=12 * collected.size,
+            transcendentals=0,
+        ),
+    )(collected, wave, linear)
+
+
+def dot_rows(left, right):
+    return lax.dot_general(
+        left, right, (((1,), (1,)), ((), ())), preferred_element_type=jnp.float32
+    )
+
+
+def first_kernel(vector_ref, wave_ref, cos_ref, sin_ref, out_ref, high_ref, low_ref):
+    _, bins, nodes, inner = vector_ref.shape
+
+    @pl.when(pl.program_id(0) == 0)
+    def _():
+        high, low = split(wave_ref[...])
+        high_ref[...] = high
+        low_ref[...] = low
+
+    for t in range(0, bins, 2):
+        row = jnp.concatenate(
+            [vector_ref[c, t : t + 2].reshape(2 * nodes, inner) for c in range(2)], axis=1
+        )
+        high, low = split(row)
+        total = dot_rows(low_ref[...], high) + dot_rows(high_ref[...], low)
+        total = total + dot_rows(high_ref[...], high)
+        for h in range(2):
+            real = total[:inner, h * nodes : (h + 1) * nodes]
+            imag = total[inner:, h * nodes : (h + 1) * nodes]
+            cos = cos_ref[0, :, t + h : t + h + 1]
+            sin = sin_ref[0, :, t + h : t + h + 1]
+            out_ref[:, 0, t + h, :] = real * cos - imag * sin
+            out_ref[:, 1, t + h, :] = real * sin + imag * cos
+
+
+def first_stage(vector, wave, cos, sin):
+    _, bins, nodes, inner = vector.shape
+    tile = 8
+    tiled = [part.reshape(inner, bins // tile, tile).transpose(1, 0, 2) for part in (cos, sin)]
+    return pl.pallas_call(
+        first_kernel,
+        grid=(bins // tile,),
+        in_specs=[
+            pl.BlockSpec((2, tile, nodes, inner), lambda i: (0, i, 0, 0)),
+            pl.BlockSpec((2 * inner, 2 * inner), lambda i: (0, 0)),
+            pl.BlockSpec((1, inner, tile), lambda i: (i, 0, 0)),
+            pl.BlockSpec((1, inner, tile), lambda i: (i, 0, 0)),
+        ],
+        out_specs=pl.BlockSpec((inner, 2, tile, nodes), lambda i: (0, 0, i, 0)),
+        out_shape=jax.ShapeDtypeStruct((inner, 2, bins, nodes), jnp.float32),
+        scratch_shapes=[
+            pltpu.VMEM((2 * inner, 2 * inner), jnp.bfloat16),
+            pltpu.VMEM((2 * inner, 2 * inner), jnp.bfloat16),
+        ],
+        compiler_params=pltpu.CompilerParams(vmem_limit_bytes=32 * 1024 * 1024),
+        cost_estimate=pl.CostEstimate(
+            flops=6 * bins * nodes * 4 * inner * inner,
+            bytes_accessed=8 * vector.size,
+            transcendentals=0,
+        ),
+    )(vector, wave, *tiled)
 
 
 def body(
@@ -53,31 +181,36 @@
     outer_fore = wave(outer_cos, -outer_sin)
 
     def inverse_first(vector):
-        mixed = contract("canb,cbem->eman", vector, inner_back)
-        cos, sin = back_cos[:, :, None], back_sin[:, :, None]
-        return jnp.stack(
-            [mixed[0] * cos - mixed[1] * sin, mixed[0] * sin + mixed[1] * cos]
-        )
+        rows = inner_back.transpose(2, 3, 0, 1).reshape(2 * inner_size, 2 * inner_size)
+        return first_stage(vector, rows, back_cos, back_sin)
 
     def inverse_exchange(twisted):
-        return lax.all_to_all(twisted, "freq", split_axis=1, concat_axis=2, tiled=True)
+        return lax.all_to_all(twisted, "freq", split_axis=0, concat_axis=0, tiled=True)
 
     def inverse_second(spread):
-        return contract("cman,cael->emnl", spread, outer_back)
+        parts = spread.reshape(freq_count, local_steps, 2, local_bins, node_dev)
+        joined = parts.transpose(2, 1, 0, 3, 4).reshape(
+            2, local_steps, outer_size, node_dev
+        )
+        return contract("cman,cael->emnl", joined, outer_back)
 
     def forward_first(current):
         stamped = contract("cmdl,nd->cmnl", current, incidence)
-        turned = contract("cmnl,clea->eman", stamped, outer_fore)
-        cos, sin = fore_cos[:, :, None], fore_sin[:, :, None]
-        return jnp.stack(
-            [turned[0] * cos + turned[1] * sin, turned[1] * cos - turned[0] * sin]
-        )
+        turned = contract("cmnl,clea->eamn", stamped, outer_fore)
+        cos, sin = fore_cos.T[:, :, None], fore_sin.T[:, :, None]
+        twisted = jnp.stack(
+            [turned[0] * cos + turned[1] * sin, turned[1] * cos - turned[0] * sin], axis=1
+        )
+        return with_layout_constraint(twisted, Layout(major_to_minor=(0, 1, 2, 3)))
 
     def forward_exchange(twisted):
-        return lax.all_to_all(twisted, "freq", split_axis=2, concat_axis=1, tiled=True)
-
-    def forward_second(collected):
-        return contract("cman,cmeb->eanb", collected, inner_fore)
+        return lax.all_to_all(twisted, "freq", split_axis=0, concat_axis=0, tiled=True)
+
+    def forward_second(collected, linear_part):
+        parts = collected.reshape(freq_count, local_bins, 2, local_steps, node_dev)
+        return last_stage(
+            parts, inner_fore.reshape(2 * inner_size, 2 * inner_size), linear_part
+        )
 
     def arrange(values, axis):
         return jnp.concatenate(
@@ -156,9 +289,8 @@
     vector_one, vector_two, collected_one = lax.optimization_barrier(
         (first_vector, second_vector, collected_one)
     )
-    first_product = linear(vector_one) + forward_second(collected_one)
-    second_linear = linear(vector_two)
-    second_product = second_linear + forward_second(collected_two)
+    first_product = forward_second(collected_one, linear(vector_one))
+    second_product = forward_second(collected_two, linear(vector_two))
     return (first_product, second_product)
 
 

time: 867 us -> 813 us (0.938)
  Pallas kernels: 0 us -> 53.9 us
  local copies, waits for them, and re-layouts: 111 us -> 59 us
  matrix products: 178 us -> 137 us
  waiting for transfers between devices: 509 us -> 475 us
  other arithmetic: 29.3 us -> 47.8 us
    pallas_call x0 -> x4, Pallas kernels: none -> 53.9 us  [the longest x2 28.7 us: first_stage(): pl.pallas_call(first_kernel, grid=(bins // tile,), in_specs=[pl.BlockSpec...]
    dot_general x30 -> x26, matrix products: 177 us -> 136 us  [contract(): return jnp.einsum(form, left, right, precision=precise)]
    all_to_all x4, waiting for transfers between devices: 363 us -> 325 us  [the longest x2 182 us: inverse_exchange(): lax.all_to_all(twisted, 'freq', split_axis=0, concat_axis=0, tiled=True)]
    all_to_all x4 -> x0, local copies, waits for them, and re-layouts: 29.9 us -> none  [the longest x2 16.9 us: inverse_exchange(): lax.all_to_all(twisted, 'freq', split_axis=1, concat_axis=2, tiled=True)]
    optimization_barrier x3 -> x0, local copies, waits for them, and re-layouts: 24.6 us -> none  [the longest x1 8.25 us: body(): lax.optimization_barrier((spread_one, twisted_two))]
    add x2, other arithmetic: 5.93 us -> 18.7 us  [forward_first(): turned[0] * cos + turned[1] * sin]
    transpose x0 -> x3, local copies, waits for them, and re-layouts: none -> 9.7 us  [the longest x2 8.89 us: inverse_second(): parts.transpose(2, 1, 0, 3, 4).reshape(2, local_steps, outer_size, node_dev)]
    unnamed x56 -> x62, local copies, waits for them, and re-layouts: 20.8 us -> 17.8 us
  transfers between devices with their start and end apart: 10 -> 10, of which waited for: 10 -> 8; matrix products, arithmetic and copies ran while one was open for 25% -> 27% of each run, Pallas kernels for 0% -> 3%
where the time goes in v2:
time: 813 us; the launch traced here: 803 us
  waiting for transfers between devices  475 us (58%)
  matrix products  137 us (17%)
  local copies, waits for them, and re-layouts  59 us (7%)
  Pallas kernels  53.9 us (7%)
  other arithmetic  47.8 us (6%)
  starting transfers between devices  28.9 us (4%)
    all_to_all x2, waiting for transfers between devices, inverse_exchange(): lax.all_to_all(twisted, 'freq', split_axis=0, concat_axis=0, tiled=True)  182 us
    ppermute x6, waiting for transfers between devices, middle(): block = lax.ppermute(block, 'node', pairs)  150 us
    all_to_all x2, waiting for transfers between devices, forward_exchange(): lax.all_to_all(twisted, 'freq', split_axis=0, concat_axis=0, tiled=True)  143 us
    dot_general x26, matrix products, contract(): return jnp.einsum(form, left, right, precision=precise)  136 us
    pallas_call x2, Pallas kernels, first_stage(): pl.pallas_call(first_kernel, grid=(bins // tile,), in_specs=[pl.BlockSpec...  28.7 us
    pallas_call x2, Pallas kernels, last_stage(): pl.pallas_call(last_kernel, grid=(bins // tile,), in_specs=[pl.BlockSpec(...  25.2 us
    add x2, other arithmetic, forward_first(): turned[0] * cos + turned[1] * sin  18.7 us
    optimization_barrier x2, local copies, waits for them, and re-layouts, body(): lax.optimization_barrier((first_vector, second_vector, collected_one))  17.9 us
  transfers between devices with their start and end apart: 10, of which 8 were waited for; matrix products, arithmetic and copies ran while one was open for 27% of the time, Pallas kernels for 3%

profile of v2, /device:TPU:0, one launch (start us, length us, event | category | flops | bytes accessed | tf_op | source)
XLA Modules:
  0.0 803.1 jit_solution(10795621768580920830)
XLA Ops:
  6.0 2.8 multiply_sine_fusion
  8.8 3.4 copy-done.3
  12.2 14.4 %shard_map.86 = f32[256,2,32,128]{3,2,1,0:T(8,128)S(1)} custom-call(f32[2,32,128,256]{3,2,1,0:T(8,128)S(1)} %copy-done.3, f32[512,512]{1,0:T(8,128)S(1)} %bitcast.305, f32[4,256,8]{2,1,0:T(8,128)S(1)} %get-tuple-element.43.cos_ref, f32[4,256,8]{2,1,0:T(8,128)S(1)} %get-tuple-element.42.sin_ref), custom_call_target="tpu_custom_call" | custom-call | flops 6442450944 | bytes 16777216 | tf_op jit(solution)/shard_map/pallas_call | solution.py:126
  26.5 3.4 copy-done.5
  29.9 6.3 all-to-all-start
  36.3 3.4 copy-done.2
  39.6 14.4 %shard_map.87 = f32[256,2,32,128]{3,2,1,0:T(8,128)S(1)} custom-call(f32[2,32,128,256]{3,2,1,0:T(8,128)S(1)} %copy-done.2, f32[512,512]{1,0:T(8,128)S(1)} %bitcast.306, f32[4,256,8]{2,1,0:T(8,128)S(1)} %get-tuple-element.43.cos_ref, f32[4,256,8]{2,1,0:T(8,128)S(1)} %get-tuple-element.42.sin_ref), custom_call_target="tpu_custom_call" | custom-call | flops 6442450944 | bytes 16777216 | tf_op jit(solution)/shard_map/pallas_call | solution.py:126
  54.0 3.4 copy-done.4
  57.4 162.8 %all-to-all-done = f32[256,2,32,128]{3,2,1,0:T(8,128)} async-done(((f32[256,2,32,128]{3,2,1,0:T(8,128)}), f32[256,2,32,128]{3,2,1,0:T(8,128)}, u32[]{:S(2)}, u32[]{:S(2)}) %all-to-all-start) | async-done | bytes 8388640 | tf_op jit(solution)/shard_map/all_to_all | solution.py:188
  220.3 5.2 all-to-all-start.1
  227.4 6.9 constant_dynamic-slice_fusion.7
  234.3 4.4 copy.42
  238.7 7.4 fusion.80
  246.2 4.2 fusion.57
  250.4 1.5 collective-permute-start
  251.9 4.6 fusion.60
  256.5 1.5 collective-permute-start.1
  258.1 4.3 fusion.63
  265.0 2.5 slice_bitcast_fusion.5
  267.5 4.2 fusion.54
  271.8 7.1 fusion.20
  278.9 20.3 %collective-permute-done = f32[2,32,32,256]{3,2,1,0:T(8,128)} collective-permute-done((f32[2,32,32,256]{3,2,1,0:T(8,128)}, f32[2,32,32,256]{3,2,1,0:T(8,128)}, u32[]{:S(2)}, u32[]{:S(2)}) %collective-permute-start) | collective-permute-done | bytes 2097184 | tf_op jit(solution)/shard_map/ppermute | solution.py:244
  299.2 50.2 %collective-permute-done.1 = f32[2,32,32,256]{3,2,1,0:T(8,128)} collective-permute-done((f32[2,32,32,256]{3,2,1,0:T(8,128)}, f32[2,32,32,256]{3,2,1,0:T(8,128)}, u32[]{:S(2)}, u32[]{:S(2)}) %collective-permute-start.1) | collective-permute-done | bytes 2097184 | tf_op jit(solution)/shard_map/ppermute | solution.py:244
  349.4 11.7 %fusion.1 = f32[2,32,128,256]{3,2,1,0:T(8,128)} fusion(f32[2,32,32,256]{3,2,1,0:T(8,128)} %collective-permute-done.2, f32[2,32,32,256]{3,2,1,0:T(8,128)} %collective-permute-done.1, f32[2,32,32,256]{3,2,1,0:T(8,128)} %collective-permute-done, f32[2,32,32,256]{3,2,1,0:T(8,128)} %fusion.54, f32[128,2,32,256]{3,0,2,1:T(8,128)} %fusion.20, ...), kind=kOutput, calls=%fused_computation.3 | convolution fusion | flops 1625325568 | bytes 41943552 | tf_op jit(solution)/shard_map/cmnl,nd->cmdl/dot_general | solution.py:15
  361.1 6.4 fusion.34
  367.5 7.6 fusion.48
  376.2 9.1 %multiply_add_fusion.1 = (f32[256,1,32,128]{3,2,1,0:T(8,128)S(1)}, f32[256,1,32,128]{3,2,1,0:T(8,128)S(1)}) fusion(f32[1,256,32,128]{3,1,2,0:T(8,128)S(1)} %get-tuple-element.29, f32[1,256,32,128]{3,1,2,0:T(8,128)S(1)} %get-tuple-element.28, f32[256,32]{1,0:T(8,128)S(1)} %copy-done.21, f32[256,32]{1,0:T(8,128)S(1)} %get-tuple-element.56), kind=kLoop, calls=%fused_computation.62 | loop fusion | flops 6291456 | bytes 16842752 | tf_op jit(solution)/shard_map/add | solution.py:202
  385.3 4.4 pad_maximum_fusion.1
  389.7 19.4 %all-to-all-done.1 = f32[256,2,32,128]{3,2,1,0:T(8,128)} async-done(((f32[256,2,32,128]{3,2,1,0:T(8,128)}), f32[256,2,32,128]{3,2,1,0:T(8,128)}, u32[]{:S(2)}, u32[]{:S(2)}) %all-to-all-start.1) | async-done | bytes 8388640 | tf_op jit(solution)/shard_map/all_to_all | solution.py:188
  409.2 5.3 all-to-all-start.2
  414.5 4.5 copy.49
  419.0 7.4 fusion.78
  426.5 2.9 fusion.69
  429.4 3.1 fusion.72
  432.5 2.9 fusion.75
  435.5 1.6 collective-permute-start.3
  437.1 1.5 collective-permute-start.4
  439.1 4.3 fusion.66
  443.4 7.1 fusion.8
  450.5 33.6 %collective-permute-done.3 = f32[2,32,32,256]{3,2,1,0:T(8,128)} collective-permute-done((f32[2,32,32,256]{3,2,1,0:T(8,128)S(1)}, f32[2,32,32,256]{3,2,1,0:T(8,128)}, u32[]{:S(2)}, u32[]{:S(2)}) %collective-permute-start.3) | collective-permute-done | bytes 2097184 | tf_op jit(solution)/shard_map/ppermute | solution.py:244
  484.1 45.6 %collective-permute-done.4 = f32[2,32,32,256]{3,2,1,0:T(8,128)} collective-permute-done((f32[2,32,32,256]{3,2,1,0:T(8,128)S(1)}, f32[2,32,32,256]{3,2,1,0:T(8,128)}, u32[]{:S(2)}, u32[]{:S(2)}) %collective-permute-start.4) | collective-permute-done | bytes 2097184 | tf_op jit(solution)/shard_map/ppermute | solution.py:244
  529.7 11.5 %fusion.3 = f32[2,32,128,256]{3,2,1,0:T(8,128)} fusion(f32[2,32,32,256]{3,2,1,0:T(8,128)} %collective-permute-done.5, f32[2,32,32,256]{3,2,1,0:T(8,128)} %collective-permute-done.4, f32[2,32,32,256]{3,2,1,0:T(8,128)} %collective-permute-done.3, f32[2,32,32,256]{3,2,1,0:T(8,128)} %fusion.66, f32[128,2,32,256]{3,0,2,1:T(8,128)} %fusion.8, ...), kind=kOutput, calls=%fused_computation.7 | convolution fusion | flops 1625325568 | bytes 41943552 | tf_op jit(solution)/shard_map/cmnl,nd->cmdl/dot_general | solution.py:15
  541.2 6.6 fusion.32
  547.9 7.6 fusion.51
  556.5 9.6 %multiply_add_fusion = (f32[256,1,32,128]{3,2,1,0:T(8,128)S(1)}, f32[256,1,32,128]{3,2,1,0:T(8,128)S(1)}) fusion(f32[1,256,32,128]{3,1,2,0:T(8,128)S(1)} %get-tuple-element.27, f32[1,256,32,128]{3,1,2,0:T(8,128)S(1)} %get-tuple-element.26, f32[256,32]{1,0:T(8,128)S(1)} %copy-done.22, f32[256,32]{1,0:T(8,128)S(1)} %get-tuple-element.56), kind=kLoop, calls=%fused_computation.60 | loop fusion | flops 6291456 | bytes 16842752 | tf_op jit(solution)/shard_map/add | solution.py:202
  566.1 4.3 pad_maximum_fusion.2
  570.4 27.6 %all-to-all-done.2 = f32[256,2,32,128]{3,2,1,0:T(8,128)} async-done(((f32[256,2,32,128]{3,2,1,0:T(8,128)}), f32[256,2,32,128]{3,2,1,0:T(8,128)}, u32[]{:S(2)}, u32[]{:S(2)}) %all-to-all-start.2) | async-done | bytes 8388640 | tf_op jit(solution)/shard_map/all_to_all | solution.py:207
  598.0 5.0 all-to-all-start.3
  605.0 8.9 %copy.62 = f32[2,32,128,256]{2,3,1,0:T(8,128)} copy(f32[2,32,128,256]{3,2,1,0:T(8,128)} %vector_ref.2) | data formatting | bytes 16777216 | tf_op jit(solution)/shard_map/optimization_barrier | solution.py:289
  613.9 9.0 %copy.54 = f32[2,32,128,256]{2,3,1,0:T(8,128)} copy(f32[2,32,128,256]{3,2,1,0:T(8,128)} %vector_ref.1) | data formatting | bytes 16777216 | tf_op jit(solution)/shard_map/optimization_barrier | solution.py:289
  623.0 4.2 fusion.41
  627.6 4.2 subtract_bitcast_fusion
  631.9 1.9 fusion.40
  633.8 4.2 add_bitcast_fusion
  638.0 7.9 pad_maximum_fusion.4.linear_ref
  645.9 1.9 fusion.37
  647.8 2.5 subtract_bitcast_fusion.1
  650.3 1.9 fusion.36
  652.2 4.2 add_bitcast_fusion.1
  656.4 2.9 pad_maximum_fusion.3.linear_ref
  659.4 12.6 %shard_map.88 = f32[2,32,128,256]{3,2,1,0:T(8,128)} custom-call(f32[8,32,2,32,128]{4,3,2,1,0:T(8,128)} %bitcast.81.collected_ref, f32[512,512]{1,0:T(8,128)S(1)} %bitcast.303, f32[2,32,128,256]{3,2,1,0:T(8,128)S(1)} %pad_maximum_fusion.3.linear_ref), custom_call_target="tpu_custom_call" | custom-call | flops 6442450944 | bytes 25165824 | tf_op jit(solution)/shard_map/pallas_call | solution.py:68
  672.0 114.9 %all-to-all-done.3 = f32[256,2,32,128]{3,2,1,0:T(8,128)} async-done(((f32[256,2,32,128]{3,2,1,0:T(8,128)}), f32[256,2,32,128]{3,2,1,0:T(8,128)}, u32[]{:S(2)}, u32[]{:S(2)}) %all-to-all-start.3) | async-done | bytes 8388640 | tf_op jit(solution)/shard_map/all_to_all | solution.py:207
  786.9 3.4 copy-done.1
  790.3 12.6 %shard_map.89 = f32[2,32,128,256]{3,2,1,0:T(8,128)} custom-call(f32[8,32,2,32,128]{4,3,2,1,0:T(8,128)} %bitcast.93.collected_ref, f32[512,512]{1,0:T(8,128)S(1)} %bitcast.304, f32[2,32,128,256]{3,2,1,0:T(8,128)S(1)} %copy-done.1), custom_call_target="tpu_custom_call" | custom-call | flops 6442450944 | bytes 25165824 | tf_op jit(solution)/shard_map/pallas_call | solution.py:68
  (94 shorter events, 14.5 us)
Async XLA Ops:
  0.6 602.4 %copy-start = (f32[4,3,32,32]{3,2,1,0:T(8,128)S(1)}, f32[4,3,32,32]{3,2,1,0:T(8,128)}, u32[]{:S(2)}) copy-start(f32[4,3,32,32]{3,2,1,0:T(8,128)} %param.12) | copy-start | bytes 147460
  3.9 234.8 %copy-start.11 = (f32[1,256,2,256]{1,3,0,2:T(8,128)}, f32[1,256,2,256]{1,3,0,2:T(8,128)S(1)}, u32[]{:S(2)}) copy-start(f32[1,256,2,256]{1,3,0,2:T(8,128)S(1)} %get-tuple-element.39) | copy-start | bytes 1572868
  3.9 234.8 %copy-start.13 = (f32[1,256,2,256]{1,3,0,2:T(8,128)}, f32[1,256,2,256]{1,3,0,2:T(8,128)S(1)}, u32[]{:S(2)}) copy-start(f32[1,256,2,256]{1,3,0,2:T(8,128)S(1)} %get-tuple-element.44) | copy-start | bytes 1572868
  8.8 3.4 copy-start.3
  26.5 3.4 copy-start.5
  29.9 190.3 %all-to-all-start = ((f32[256,2,32,128]{3,2,1,0:T(8,128)}), f32[256,2,32,128]{3,2,1,0:T(8,128)}, u32[]{:S(2)}, u32[]{:S(2)}) async-start(f32[256,2,32,128]{3,2,1,0:T(8,128)} %copy-done.5), calls=%async_computation | async-start | bytes 16777216 | tf_op jit(solution)/shard_map/all_to_all | solution.py:188
  36.3 3.4 copy-start.2
  54.0 3.4 copy-start.4
  57.4 168.1 %copy-start.24 = (s32[512,3]{0,1:T(4,128)S(1)}, s32[512,3]{0,1:T(4,128)}, u32[]{:S(2)}) copy-start(s32[512,3]{0,1:T(4,128)} %param.10) | copy-start | bytes 18436
  220.3 188.9 %all-to-all-start.1 = ((f32[256,2,32,128]{3,2,1,0:T(8,128)}), f32[256,2,32,128]{3,2,1,0:T(8,128)}, u32[]{:S(2)}, u32[]{:S(2)}) async-start(f32[256,2,32,128]{3,2,1,0:T(8,128)} %copy-done.4), calls=%async_computation.1 | async-start | bytes 16777216 | tf_op jit(solution)/shard_map/all_to_all | solution.py:188
  225.6 0.6 copy-start.26
  250.4 12.5 %copy-start.19 = (f32[1,256,2,256]{1,3,2,0:T(8,128)S(1)}, f32[1,256,2,256]{1,3,2,0:T(8,128)}, u32[]{:S(2)}) copy-start(f32[1,256,2,256]{1,3,2,0:T(8,128)} %get-tuple-element.38) | copy-start | bytes 1572868
  250.4 12.5 %copy-start.20 = (f32[1,256,2,256]{1,3,2,0:T(8,128)S(1)}, f32[1,256,2,256]{1,3,2,0:T(8,128)}, u32[]{:S(2)}) copy-start(f32[1,256,2,256]{1,3,2,0:T(8,128)} %get-tuple-element.45) | copy-start | bytes 1572868
  250.4 48.8 %collective-permute-start = (f32[2,32,32,256]{3,2,1,0:T(8,128)}, f32[2,32,32,256]{3,2,1,0:T(8,128)}, u32[]{:S(2)}, u32[]{:S(2)}) collective-permute-start(f32[2,32,32,256]{3,2,1,0:T(8,128)} %fusion.57), channel_id=1, source_target_pairs={{0,8},{8,0},{16,24},{24,16},{1,9},{9,1},{17,25},{25,17},{2,10},{10... | collective-permute-start | bytes 6291464 | tf_op jit(solution)/shard_map/ppermute | solution.py:244
  256.5 7.8 copy-start.15
  256.5 7.8 copy-start.16
  256.5 7.8 copy-start.17
  256.5 92.9 %collective-permute-start.1 = (f32[2,32,32,256]{3,2,1,0:T(8,128)}, f32[2,32,32,256]{3,2,1,0:T(8,128)}, u32[]{:S(2)}, u32[]{:S(2)}) collective-permute-start(f32[2,32,32,256]{3,2,1,0:T(8,128)} %fusion.60), channel_id=1, source_target_pairs={{0,16},{8,24},{16,0},{24,8},{1,17},{9,25},{17,1},{25,9},{2,18},{10... | collective-permute-start | bytes 6291464 | tf_op jit(solution)/shard_map/ppermute | solution.py:244
  262.4 87.0 %collective-permute-start.2 = (f32[2,32,32,256]{3,2,1,0:T(8,128)}, f32[2,32,32,256]{3,2,1,0:T(8,128)}, u32[]{:S(2)}, u32[]{:S(2)}) collective-permute-start(f32[2,32,32,256]{3,2,1,0:T(8,128)} %fusion.63), channel_id=1, source_target_pairs={{0,24},{8,16},{16,8},{24,0},{1,25},{9,17},{17,9},{25,1},{2,26},{10... | collective-permute-start | bytes 6291464 | tf_op jit(solution)/shard_map/ppermute | solution.py:244
  267.5 81.9 %copy-start.6 = (f32[32,128,256]{2,1,0:T(8,128)}, f32[32,128,256]{2,1,0:T(8,128)S(1)}, u32[]{:S(2)}) copy-start(f32[32,128,256]{2,1,0:T(8,128)S(1)} %get-tuple-element.30) | copy-start | bytes 12582916
  361.1 6.4 copy-start.9
  375.2 1.0 copy-start.21
  409.2 188.8 %all-to-all-start.2 = ((f32[256,2,32,128]{3,2,1,0:T(8,128)}), f32[256,2,32,128]{3,2,1,0:T(8,128)}, u32[]{:S(2)}, u32[]{:S(2)}) async-start(f32[256,2,32,128]{3,2,1,0:T(8,128)} %pad_maximum_fusion.1), calls=%async_computation.2 | async-start | bytes 16777216 | tf_op jit(solution)/shard_map/all_to_all | solution.py:207
  414.5 4.5 copy-start.12
  414.5 4.5 copy-start.14
  435.5 48.6 %collective-permute-start.3 = (f32[2,32,32,256]{3,2,1,0:T(8,128)S(1)}, f32[2,32,32,256]{3,2,1,0:T(8,128)}, u32[]{:S(2)}, u32[]{:S(2)}) collective-permute-start(f32[2,32,32,256]{3,2,1,0:T(8,128)S(1)} %fusion.69), channel_id=1, source_target_pairs={{0,8},{8,0},{16,24},{24,16},{1,9},{9,1},{17,25},{25,17},{2,10},{10... | collective-permute-start | bytes 6291464 | tf_op jit(solution)/shard_map/ppermute | solution.py:244
  437.1 92.6 %collective-permute-start.4 = (f32[2,32,32,256]{3,2,1,0:T(8,128)S(1)}, f32[2,32,32,256]{3,2,1,0:T(8,128)}, u32[]{:S(2)}, u32[]{:S(2)}) collective-permute-start(f32[2,32,32,256]{3,2,1,0:T(8,128)S(1)} %fusion.72), channel_id=1, source_target_pairs={{0,16},{8,24},{16,0},{24,8},{1,17},{9,25},{17,1},{25,9},{2,18},{10... | collective-permute-start | bytes 6291464 | tf_op jit(solution)/shard_map/ppermute | solution.py:244
  438.6 91.1 %collective-permute-start.5 = (f32[2,32,32,256]{3,2,1,0:T(8,128)S(1)}, f32[2,32,32,256]{3,2,1,0:T(8,128)}, u32[]{:S(2)}, u32[]{:S(2)}) collective-permute-start(f32[2,32,32,256]{3,2,1,0:T(8,128)S(1)} %fusion.75), channel_id=1, source_target_pairs={{0,24},{8,16},{16,8},{24,0},{1,25},{9,17},{17,9},{25,1},{2,26},{10... | collective-permute-start | bytes 6291464 | tf_op jit(solution)/shard_map/ppermute | solution.py:244
  443.4 86.3 %copy-start.7 = (f32[32,128,256]{2,1,0:T(8,128)S(1)}, f32[32,128,256]{2,1,0:T(8,128)}, u32[]{:S(2)}) copy-start(f32[32,128,256]{2,1,0:T(8,128)} %copy-done.6) | copy-start | bytes 12582916
  541.2 6.6 copy-start.10
  555.5 1.0 copy-start.22
  570.4 32.6 %copy-start.25 = (s32[4,3]{1,0:T(4,128)S(1)}, s32[4,3]{1,0:T(4,128)}, u32[]{:S(2)}) copy-start(s32[4,3]{1,0:T(4,128)} %param.11) | copy-start | bytes 148
  570.4 33.2 %copy-start.23 = (f32[4,3,32,32]{3,2,1,0:T(8,128)S(1)}, f32[4,3,32,32]{3,2,1,0:T(8,128)}, u32[]{:S(2)}) copy-start(f32[4,3,32,32]{3,2,1,0:T(8,128)} %param.13) | copy-start | bytes 147460
  570.4 33.9 %copy-start.18 = (f32[2,256,2,256]{1,3,2,0:T(8,128)S(1)}, f32[2,256,2,256]{1,3,2,0:T(8,128)}, u32[]{:S(2)}) copy-start(f32[2,256,2,256]{1,3,2,0:T(8,128)} %get-tuple-element.36) | copy-start | bytes 3145732
  570.4 34.6 %copy-start.27 = (s32[32]{0:T(128)S(1)}, s32[32]{0:T(128)}, u32[]{:S(2)}) copy-start(s32[32]{0:T(128)} %copy-done.26) | copy-start | bytes 388
  598.0 188.9 %all-to-all-start.3 = ((f32[256,2,32,128]{3,2,1,0:T(8,128)}), f32[256,2,32,128]{3,2,1,0:T(8,128)}, u32[]{:S(2)}, u32[]{:S(2)}) async-start(f32[256,2,32,128]{3,2,1,0:T(8,128)} %pad_maximum_fusion.2), calls=%async_computation.3 | async-start | bytes 16777216 | tf_op jit(solution)/shard_map/all_to_all | solution.py:207
  623.0 4.6 copy-start.8
  633.8 12.0 %slice-start = ((s8[8388608]{0:T(1024)(128)(4,1)}), s8[4194304]{0:T(1024)(128)(4,1)S(1)}, s32[]{:S(2)}) async-start(s8[8388608]{0:T(1024)(128)(4,1)} %bitcast.307), calls=%async_computation.4 | async-start | bytes 8388608
  638.0 7.9 slice-start.1
  786.9 3.4 copy-start.1
